TPU v7x, 32 devices: a whole 2x2x4 slice. The times are simulated.
32 devices in a mesh: groups: 2 (over y), row: 8 (over z, x), col: 2 (over core).
Axes of the slice: x: 2, y: 2, z: 4, core: 2. Of those that a mesh axis runs over, the one named last changes fastest.
Arguments:
- blocks: bfloat16 [16, 2, 128, 128, 128], P(('groups', 'row'), 'col'), parts along dimension 0, may hold values from -0.09375 to 0.09375
- block_rows: int32 [16, 2, 128], P(('groups', 'row'), 'col'), parts along dimension 0, may hold values from 0 to 7
- block_cols: int32 [16, 2, 128], P(('groups', 'row'), 'col'), parts along dimension 0, may hold values from 0 to 63, as said below
- block_counts: int32 [16, 2], P(('groups', 'row'), 'col'), parts along dimension 0, may hold values from 96 to 128
- primal: float32 [256, 128], P(('groups', 'col', 'row')), parts along dimension 0, may hold values from -3 to 3
- primal_bar: float32 [256, 128], P(('groups', 'col', 'row')), parts along dimension 0, may hold values from -3 to 3
- dual: float32 [128, 128], P(('groups', 'row', 'col')), parts along dimension 0, may hold values from -5 to 5
- rhs: float32 [128, 128], P(('groups', 'row', 'col')), parts along dimension 0, may hold values from -5 to 5
- cost_vec: float32 [256, 128], P(('groups', 'col', 'row')), parts along dimension 0, may hold values from -5 to 5
- lower: float32 [256, 128], P(('groups', 'col', 'row')), parts along dimension 0, may hold values from -1 to -0.1
- upper: float32 [256, 128], P(('groups', 'col', 'row')), parts along dimension 0, may hold values from 0.1 to 1
- bound_kind: int32 [256, 128], P(('groups', 'col', 'row')), parts along dimension 0, may hold values from 0 to 3
- row_kind: int32 [128, 128], P(('groups', 'row', 'col')), parts along dimension 0, may hold values from 0 to 1
- primal_step: float32 [2], P('groups'), parts along dimension 0, may hold values from 0.3 to 1
- dual_step: float32 [2], P('groups'), parts along dimension 0, may hold values from 0.3 to 1
Outputs:
- dual_new: float32 [128, 128], P(('groups', 'row', 'col')), parts along dimension 0
- primal_new: float32 [256, 128], P(('groups', 'col', 'row')), parts along dimension 0
- primal_bar_new: float32 [256, 128], P(('groups', 'col', 'row')), parts along dimension 0
There are 2 independent parts, one for each index of `groups`. A program takes and returns all parts, laid end to end along the dimension named above; each array names one. Nothing has to cross between parts.
Inputs may be any that keep to these rules, and one draw needn't show every extreme that they name: Among the live slots of one device, each owner block_cols // 8 is named at most 16 times; in every draw one owner is named exactly 16 times by the live slots of every device.
All inputs are finite; a program needn't handle non-finite values.
Results may differ from a plain program's by a relative error of at most 0.0018.
Values may be sent and summed in bfloat16 or wider, within the bound.
A program may use at most 64 MiB of HBM per device.

v0:
```python
import jax
import jax.numpy as jnp
from jax import lax
from jax.sharding import PartitionSpec as P


def body(
    blocks,
    block_rows,
    block_cols,
    block_counts,
    primal,
    primal_bar,
    dual,
    rhs,
    cost_vec,
    lower,
    upper,
    bound_kind,
    row_kind,
    primal_step,
    dual_step,
):
    matrix = blocks[0, 0]
    rows = block_rows[0, 0]
    cols = block_cols[0, 0]
    slots = matrix.shape[0]
    live = jnp.arange(slots) < block_counts[0, 0]
    n_col = lax.axis_size("col")
    shard_blocks = dual.shape[0]
    row_blocks = shard_blocks * n_col
    piece_blocks = primal.shape[0]
    gathered = lax.all_gather(primal_bar.astype(jnp.bfloat16), "row", axis=0, tiled=True)
    picked = gathered[cols]
    prod = jnp.einsum("nij,nj->ni", matrix, picked, preferred_element_type=jnp.float32)
    prod = jnp.where(live[:, None], prod, 0.0)
    row_onehot = (jnp.arange(row_blocks)[:, None] == rows[None, :]).astype(jnp.float32)
    partial_value = jnp.dot(row_onehot, prod, precision=lax.Precision.HIGHEST)
    share = lax.psum_scatter(partial_value, "col", scatter_dimension=0, tiled=True)
    moved = dual + dual_step[0] * (rhs - share)
    dual_new = jnp.where(row_kind == 1, jnp.maximum(moved, 0.0), moved)
    dual_rows = lax.all_gather(dual_new.astype(jnp.bfloat16), "col", axis=0, tiled=True)
    picked_dual = dual_rows[rows]
    back = jnp.einsum("nij,ni->nj", matrix, picked_dual, preferred_element_type=jnp.float32)
    back = jnp.where(live[:, None], back, 0.0)
    onehot = (jnp.arange(lax.axis_size("row") * piece_blocks)[:, None] == cols[None, :]).astype(
        jnp.float32
    )
    kty = lax.psum_scatter(
        jnp.dot(onehot, back, precision=lax.Precision.HIGHEST),
        "row",
        scatter_dimension=0,
        tiled=True,
    )
    moved_primal = primal - primal_step[0] * (cost_vec - kty)
    has_lower = (bound_kind == 1) | (bound_kind == 3)
    has_upper = (bound_kind == 2) | (bound_kind == 3)
    moved_primal = jnp.where(has_lower, jnp.maximum(moved_primal, lower), moved_primal)
    primal_new = jnp.where(has_upper, jnp.minimum(moved_primal, upper), moved_primal)
    return (dual_new, primal_new, 2.0 * primal_new - primal)


def solution(mesh):
    placed = (
        P(("groups", "row"), "col", None, None, None),
        P(("groups", "row"), "col", None),
        P(("groups", "row"), "col", None),
        P(("groups", "row"), "col"),
        P(("groups", "col", "row"), None),
        P(("groups", "col", "row"), None),
        P(("groups", "row", "col"), None),
        P(("groups", "row", "col"), None),
        P(("groups", "col", "row"), None),
        P(("groups", "col", "row"), None),
        P(("groups", "col", "row"), None),
        P(("groups", "col", "row"), None),
        P(("groups", "row", "col"), None),
        P("groups"),
        P("groups"),
    )
    return jax.shard_map(
        body,
        mesh=mesh,
        in_specs=placed,
        out_specs=(
            P(("groups", "row", "col"), None),
            P(("groups", "col", "row"), None),
            P(("groups", "col", "row"), None),
        ),
        check_vma=False,
    )
```

profile of v0, /device:TPU:0, one launch (start us, length us, event | category | flops | bytes accessed | tf_op | source)
XLA Modules:
  0.0 85.2 jit_solution(14190156364572957996)
XLA Ops:
  0.6 0.0 copy-start.11
  0.7 0.7 convert_element_type.8
  1.4 27.8 %all_gather.6 = bf16[64,128]{1,0:T(8,128)(2,1)S(1)} all-gather(bf16[8,128]{1,0:T(8,128)(2,1)S(1)} %convert_element_type.8), channel_id=1, replica_groups=mesh['groups'=2,'row'=8,'col'=2] {'row'}, dimensions={0}, use_global_device_ids=true | all-gather | bytes 18432 | tf_op jit(solution)/shard_map/all_gather | solution.py:33
  29.2 0.7 fusion.20
  29.8 0.7 gather_fusion
  30.5 0.0 copy-start.10
  30.6 0.0 copy-start
  30.6 0.0 copy-start.1
  30.6 0.0 copy-start.2
  30.6 0.0 copy-start.3
  30.6 0.0 copy-start.4
  30.6 4.5 %fusion.2 = f32[128,1,128]{2,1,0:T(1,128)S(1)} fusion(bf16[1,1,128,128,128]{4,3,2,1,0:T(8,128)(2,1)} %param.15, bf16[128,128,1]{1,0,2:T(8,128)(2,1)S(1)} %bitcast.33), kind=kOutput, calls=%fused_computation.4 | convolution fusion | flops 4194304 | bytes 4292608 | tf_op jit(solution)/shard_map/nij,nj->ni/dot_general | solution.py:35
  35.8 0.2 fusion.8
  36.0 2.5 %all-reduce = f32[8,128]{1,0:T(8,128)S(1)} all-reduce(f32[8,128]{1,0:T(8,128)S(1)} %fusion.8), channel_id=2, replica_groups=mesh['groups'=2,'row'=8,'col'=2] {'col'}, use_global_device_ids=true, to_apply=%region_0.1.clone | all-reduce | flops 1024 | bytes 8192
  38.5 0.0 copy-done.11
  38.5 0.6 dynamic-slice
  40.4 0.6 convert_bitcast_fusion
  41.0 1.8 %all-gather = bf16[2,4,128]{2,1,0:T(4,128)(2,1)S(1)} all-gather(bf16[1,4,128]{2,1,0:T(4,128)(2,1)S(1)} %get-tuple-element.5), channel_id=1, replica_groups=mesh['groups'=2,'row'=8,'col'=2] {'col'}, dimensions={0}, use_global_device_ids=true | all-gather | bytes 3072 | tf_op jit(solution)/shard_map/all_gather | solution.py:42
  42.7 0.7 gather_fusion.1
  43.5 3.4 %fusion = f32[128,1,128]{2,1,0:T(1,128)S(1)} fusion(bf16[1,1,128,128,128]{4,3,2,1,0:T(8,128)(2,1)} %param.15, bf16[128,128,1]{1,0,2:T(8,128)(2,1)S(1)} %bitcast.34), kind=kOutput, calls=%fused_computation.2 | convolution fusion | flops 4194304 | bytes 4292608 | tf_op jit(solution)/shard_map/nij,ni->nj/dot_general | solution.py:44
  46.8 0.3 fusion.6
  47.1 35.6 %all-reduce.1 = f32[64,128]{1,0:T(8,128)S(1)} all-reduce(f32[64,128]{1,0:T(8,128)S(1)} %fusion.6), channel_id=3, replica_groups=mesh['groups'=2,'row'=8,'col'=2] {'row'}, use_global_device_ids=true, to_apply=%region_1.2.clone | all-reduce | flops 8192 | bytes 65536
  82.7 0.6 dynamic-slice.2
  84.6 0.6 multiply_subtract_fusion
  (20 shorter events, 0.1 us)
Async XLA Ops:
  0.6 37.8 %copy-start.11 = (u32[32]{0:T(128)S(1)}, u32[32]{0:T(128)}, u32[]{:S(2)}) copy-start(u32[32]{0:T(128)} %constant.35) | copy-start | bytes 388
  0.6 39.7 %copy-start.5 = (f32[4,128]{1,0:T(4,128)S(1)}, f32[4,128]{1,0:T(4,128)}, u32[]{:S(2)}) copy-start(f32[4,128]{1,0:T(4,128)} %param.21) | copy-start | bytes 6148
  0.7 39.7 %copy-start.6 = (f32[4,128]{1,0:T(4,128)S(1)}, f32[4,128]{1,0:T(4,128)}, u32[]{:S(2)}) copy-start(f32[4,128]{1,0:T(4,128)} %param.22) | copy-start | bytes 6148
  0.7 35.1 %copy-start.8 = (s32[1,1,128]{2,1,0:T(1,128)S(1)}, s32[1,1,128]{2,1,0:T(1,128)}, u32[]{:S(2)}) copy-start(s32[1,1,128]{2,1,0:T(1,128)} %param.16) | copy-start | bytes 1540
  0.7 39.7 %copy-start.7 = (s32[4,128]{1,0:T(4,128)S(1)}, s32[4,128]{1,0:T(4,128)}, u32[]{:S(2)}) copy-start(s32[4,128]{1,0:T(4,128)} %param.27) | copy-start | bytes 6148
  30.5 16.3 %copy-start.9 = (s32[1,1,128]{2,1,0:T(1,128)S(1)}, s32[1,1,128]{2,1,0:T(1,128)}, u32[]{:S(2)}) copy-start(s32[1,1,128]{2,1,0:T(1,128)} %param.17) | copy-start | bytes 1540
  30.5 52.1 %copy-start.10 = (u32[32]{0:T(128)S(1)}, u32[32]{0:T(128)}, u32[]{:S(2)}) copy-start(u32[32]{0:T(128)} %constant.39) | copy-start | bytes 388
  30.6 54.0 %copy-start = (f32[8,128]{1,0:T(8,128)S(1)}, f32[8,128]{1,0:T(8,128)}, u32[]{:S(2)}) copy-start(f32[8,128]{1,0:T(8,128)} %param.19) | copy-start | bytes 12292
  30.6 54.0 %copy-start.1 = (f32[8,128]{1,0:T(8,128)S(1)}, f32[8,128]{1,0:T(8,128)}, u32[]{:S(2)}) copy-start(f32[8,128]{1,0:T(8,128)} %param.25) | copy-start | bytes 12292
  30.6 54.0 %copy-start.2 = (f32[8,128]{1,0:T(8,128)S(1)}, f32[8,128]{1,0:T(8,128)}, u32[]{:S(2)}) copy-start(f32[8,128]{1,0:T(8,128)} %param.24) | copy-start | bytes 12292
  30.6 54.0 %copy-start.3 = (f32[8,128]{1,0:T(8,128)S(1)}, f32[8,128]{1,0:T(8,128)}, u32[]{:S(2)}) copy-start(f32[8,128]{1,0:T(8,128)} %param.23) | copy-start | bytes 12292
  30.6 54.0 %copy-start.4 = (s32[8,128]{1,0:T(8,128)S(1)}, s32[8,128]{1,0:T(8,128)}, u32[]{:S(2)}) copy-start(s32[8,128]{1,0:T(8,128)} %param.26) | copy-start | bytes 12292
where the time goes:
time: 85.5 us; the launch traced here: 85.2 us
  blocking collectives  67.6 us (79%)
  matrix products  8.28 us (10%)
  between operations  4.1 us (5%)
  local copies, waits for them, and re-layouts  2.65 us (3%)
  other arithmetic  2.59 us (3%)
    unnamed x2, blocking collectives  38.1 us
    all_gather x1, blocking collectives, body(): lax.all_gather(primal_bar.astype(jnp.bfloat16), 'row', axis=0, tiled=True)  27.8 us
    dot_general x1, matrix products, body(): jnp.einsum('nij,nj->ni', matrix, picked, preferred_element_type=jnp.float32)  4.46 us
    dot_general x1, matrix products, body(): jnp.einsum('nij,ni->nj', matrix, picked_dual, preferred_element_type=jnp....  3.37 us
    all_gather x1, blocking collectives, body(): lax.all_gather(dual_new.astype(jnp.bfloat16), 'col', axis=0, tiled=True)  1.77 us

commit v1 on v0

v1 whole, which is shorter than its diff:
```python
import functools

import jax
import jax.numpy as jnp
from jax import lax
from jax.experimental import pallas as pl
from jax.experimental.pallas import tpu as pltpu
from jax.sharding import PartitionSpec as P

MESH = pl.DeviceIdType.MESH
BLOCK_CHUNKS = 4


def kernel(
    n_row,
    blocks,
    block_rows,
    block_cols,
    block_counts,
    primal,
    primal_bar,
    dual,
    rhs,
    cost_vec,
    lower,
    upper,
    bound_kind,
    row_kind,
    primal_step,
    dual_step,
    dual_out,
    primal_out,
    bar_out,
    blk,
    rows_s,
    cols_s,
    count_s,
    pstep_s,
    dstep_s,
    xall,
    dual_v,
    primal_v,
    kind_row_v,
    kind_v,
    packed,
    part,
    yall,
    kty,
    pieces,
    out_d,
    out_p,
    local_sem,
    blk_sem,
    x_send,
    x_recv,
    pair_send,
    pair_recv,
    t_send,
    t_recv,
):
    r = lax.axis_index("row")
    c = lax.axis_index("col")
    slots, size = blk.shape[0], blk.shape[1]
    xb = primal.shape[0]
    yb = dual.shape[0]
    mine = pl.ds(pl.multiple_of(r * xb, xb), xb)
    per_chunk = slots // BLOCK_CHUNKS

    def local(src, dst, i):
        copy = pltpu.make_async_copy(src, dst, local_sem.at[i])
        copy.start()
        return copy

    x_copy = local(primal_bar, xall.at[mine], 0)
    dual_copies = [
        local(dual, dual_v.at[0], 1),
        local(rhs, dual_v.at[1], 2),
        local(row_kind, kind_row_v, 3),
        local(dual_step, dstep_s, 4),
    ]
    index_copies = [
        local(block_rows.at[0], rows_s, 5),
        local(block_cols.at[0], cols_s, 6),
        local(block_counts, count_s, 7),
    ]
    blk_copies = []
    for k in range(BLOCK_CHUNKS):
        span = pl.ds(k * per_chunk, per_chunk)
        copy = pltpu.make_async_copy(blocks.at[0, 0, span], blk.at[span], blk_sem.at[k])
        copy.start()
        blk_copies.append(copy)
    primal_copies = [
        local(primal, primal_v.at[0], 8),
        local(cost_vec, primal_v.at[1], 9),
        local(lower, primal_v.at[2], 10),
        local(upper, primal_v.at[3], 11),
        local(bound_kind, kind_v, 12),
        local(primal_step, pstep_s, 13),
    ]

    def peer(k):
        return lax.rem(r + k, n_row)

    def for_peers(do):
        if n_row <= 8:
            for k in range(1, n_row):
                do(k)
        else:
            lax.fori_loop(1, n_row, lambda k, carry: (do(k), carry)[1], 0)

    barrier = pltpu.get_barrier_semaphore()
    for_peers(
        lambda k: pl.semaphore_signal(
            barrier, inc=1, device_id={"row": peer(k)}, device_id_type=MESH
        )
    )
    pl.semaphore_signal(barrier, inc=1, device_id={"col": 1 - c}, device_id_type=MESH)
    pl.semaphore_wait(barrier, n_row)

    def x_remote(k):
        return pltpu.make_async_remote_copy(
            src_ref=xall.at[mine],
            dst_ref=xall.at[mine],
            send_sem=x_send.at[k],
            recv_sem=x_recv.at[k],
            device_id={"row": peer(k)},
            device_id_type=MESH,
        )

    x_copy.wait()
    for_peers(lambda k: x_remote(k).start())

    for copy in dual_copies:
        copy.wait()
    dstep = dstep_s[0]
    packed[c, 0] = dual_v[0] + dstep * dual_v[1]
    packed[c, 1] = jnp.where(kind_row_v[...] == 1, 0.0, -jnp.inf)

    def to_pair(src, dst, i):
        return pltpu.make_async_remote_copy(
            src_ref=src,
            dst_ref=dst,
            send_sem=pair_send.at[i],
            recv_sem=pair_recv.at[i],
            device_id={"col": 1 - c},
            device_id_type=MESH,
        )

    pack_copy = to_pair(packed.at[c], packed.at[c], 0)
    pack_copy.start()

    for copy in index_copies:
        copy.wait()
    count = count_s[0, 0]
    row_iota = lax.broadcasted_iota(jnp.int32, (2 * yb, size), 0)
    col_iota = lax.broadcasted_iota(jnp.int32, (xb * n_row, size), 0)
    for copy in blk_copies:
        copy.wait()
    for_peers(lambda k: x_remote(k).wait_recv())

    def picked(n):
        live_row = jnp.where(n < count, rows_s[0, n], -1)
        return jnp.where(row_iota == live_row, xall[pl.ds(cols_s[0, n], 1), :], 0.0)

    def forward(q, acc):
        n = 4 * q
        left = jnp.concatenate(
            [
                jnp.concatenate([picked(n), picked(n + 1)], 1),
                jnp.concatenate([picked(n + 2), picked(n + 3)], 1),
            ],
            0,
        ).astype(jnp.bfloat16)
        right = jnp.concatenate(
            [
                jnp.concatenate([blk[n], blk[n + 1]], 1),
                jnp.concatenate([blk[n + 2], blk[n + 3]], 1),
            ],
            0,
        )
        return acc + lax.dot_general(
            left, right, (((1,), (1,)), ((), ())), preferred_element_type=jnp.float32
        )

    acc = jnp.zeros((4 * yb, 2 * size), jnp.float32)
    acc = lax.fori_loop(0, slots // 4, forward, acc, unroll=8)
    total = acc[: 2 * yb, :size] + acc[2 * yb :, size:]
    for h in range(2):
        part[0, h] = total[h * yb : (h + 1) * yb]
    part_copy = to_pair(part.at[0], part.at[1], 1)
    part_copy.start()
    pack_copy.wait_recv()
    part_copy.wait_recv()

    for h in range(2):
        moved = packed[h, 0] - dstep * (part[0, h] + part[1, h])
        new = jnp.maximum(moved, packed[h, 1])
        out_d[h] = new
        yall[h * yb : (h + 1) * yb, :] = new.astype(jnp.bfloat16).astype(jnp.float32)
    d_copy = local(out_d.at[c], dual_out, 14)

    def masked(n):
        live_col = jnp.where(n < count, cols_s[0, n], -1)
        return jnp.where(col_iota == live_col, yall[pl.ds(rows_s[0, n], 1), :], 0.0)

    def backward(q, acc):
        n = 2 * q
        left = jnp.concatenate([masked(n), masked(n + 1)], 1).astype(jnp.bfloat16)
        right = jnp.concatenate([blk[n], blk[n + 1]], 0)
        return acc + jnp.dot(left, right, preferred_element_type=jnp.float32)

    if n_row <= 8:
        acc = jnp.zeros((xb * n_row, size), jnp.float32)
        kty[...] = lax.fori_loop(0, slots // 2, backward, acc, unroll=8)
    else:
        kty[...] = jnp.zeros_like(kty)

        def into(q, carry):
            kty[...] = backward(q, kty[...])
            return carry

        lax.fori_loop(0, slots // 2, into, 0)

    def t_remote(k):
        theirs = pl.ds(pl.multiple_of(peer(k) * xb, xb), xb)
        return pltpu.make_async_remote_copy(
            src_ref=kty.at[theirs],
            dst_ref=pieces.at[k],
            send_sem=t_send.at[k],
            recv_sem=t_recv.at[k],
            device_id={"row": peer(k)},
            device_id_type=MESH,
        )

    for_peers(lambda k: t_remote(k).start())
    for copy in primal_copies:
        copy.wait()
    total = kty[mine, :]
    if n_row <= 8:
        for k in range(1, n_row):
            t_remote(k).wait_recv()
            total = total + pieces[k]
    else:
        for_peers(lambda k: t_remote(k).wait_recv())
        total = lax.fori_loop(1, n_row, lambda k, s: s + pieces[k], total)

    old = primal_v[0]
    kind = kind_v[...]
    moved = old - pstep_s[0] * (primal_v[1] - total)
    moved = jnp.where((kind == 1) | (kind == 3), jnp.maximum(moved, primal_v[2]), moved)
    new = jnp.where((kind == 2) | (kind == 3), jnp.minimum(moved, primal_v[3]), moved)
    out_p[0] = new
    out_p[1] = 2.0 * new - old
    p_copy = local(out_p.at[0], primal_out, 15)
    b_copy = local(out_p.at[1], bar_out, 16)

    for_peers(lambda k: x_remote(k).wait_send())
    pack_copy.wait_send()
    part_copy.wait_send()
    for_peers(lambda k: t_remote(k).wait_send())
    d_copy.wait()
    p_copy.wait()
    b_copy.wait()


def body(n_row, *args):
    blocks, block_rows, primal, dual = args[0], args[1], args[4], args[6]
    slots, size = blocks.shape[2], blocks.shape[3]
    xb, yb = primal.shape[0], dual.shape[0]
    f32, i32 = jnp.float32, jnp.int32
    dma = pltpu.SemaphoreType.DMA
    return pl.pallas_call(
        functools.partial(kernel, n_row),
        out_shape=(
            jax.ShapeDtypeStruct((yb, size), f32),
            jax.ShapeDtypeStruct((xb, size), f32),
            jax.ShapeDtypeStruct((xb, size), f32),
        ),
        in_specs=[pl.BlockSpec(memory_space=pl.ANY)] * len(args),
        out_specs=[pl.BlockSpec(memory_space=pl.ANY)] * 3,
        scratch_shapes=[
            pltpu.VMEM((slots, size, size), jnp.bfloat16),
            pltpu.SMEM((1, slots), i32),
            pltpu.SMEM((1, slots), i32),
            pltpu.SMEM((1, 1), i32),
            pltpu.SMEM((1,), f32),
            pltpu.SMEM((1,), f32),
            pltpu.VMEM((n_row * xb, size), f32),
            pltpu.VMEM((2, yb, size), f32),
            pltpu.VMEM((4, xb, size), f32),
            pltpu.VMEM((yb, size), i32),
            pltpu.VMEM((xb, size), i32),
            pltpu.VMEM((2, 2, yb, size), f32),
            pltpu.VMEM((2, 2, yb, size), f32),
            pltpu.VMEM((2 * yb, size), f32),
            pltpu.VMEM((n_row * xb, size), f32),
            pltpu.VMEM((n_row, xb, size), f32),
            pltpu.VMEM((2, yb, size), f32),
            pltpu.VMEM((2, xb, size), f32),
            dma((17,)),
            dma((BLOCK_CHUNKS,)),
            dma((n_row,)),
            dma((n_row,)),
            dma((2,)),
            dma((2,)),
            dma((n_row,)),
            dma((n_row,)),
        ],
        compiler_params=pltpu.CompilerParams(
            collective_id=0, has_side_effects=True, vmem_limit_bytes=32 * 1024 * 1024
        ),
    )(*args)


def solution(mesh):
    placed = (
        P(("groups", "row"), "col", None, None, None),
        P(("groups", "row"), "col", None),
        P(("groups", "row"), "col", None),
        P(("groups", "row"), "col"),
        P(("groups", "col", "row"), None),
        P(("groups", "col", "row"), None),
        P(("groups", "row", "col"), None),
        P(("groups", "row", "col"), None),
        P(("groups", "col", "row"), None),
        P(("groups", "col", "row"), None),
        P(("groups", "col", "row"), None),
        P(("groups", "col", "row"), None),
        P(("groups", "row", "col"), None),
        P("groups"),
        P("groups"),
    )
    return jax.shard_map(
        functools.partial(body, mesh.shape["row"]),
        mesh=mesh,
        in_specs=placed,
        out_specs=(
            P(("groups", "row", "col"), None),
            P(("groups", "col", "row"), None),
            P(("groups", "col", "row"), None),
        ),
        check_vma=False,
    )
```

time: 85.5 us -> 32.8 us (0.38)
  blocking collectives: 67.6 us -> 0 us
  Pallas kernels: 0 us -> 18.3 us
  local copies, waits for them, and re-layouts: 2.65 us -> 11.4 us
  matrix products: 8.28 us -> 0 us
  other arithmetic: 2.59 us -> 0 us
  between operations: 4.1 us -> 2.6 us
    unnamed x2 -> x0, blocking collectives: 38.1 us -> none
    all_gather x2 -> x0, blocking collectives: 29.5 us -> none  [the longest x1 27.8 us: body(): lax.all_gather(primal_bar.astype(jnp.bfloat16), 'row', axis=0, tiled=True)]
    pallas_call x0 -> x1, Pallas kernels: none -> 18.3 us  [body(): pl.pallas_call(functools.partial(kernel, n_row), out_shape=(jax.ShapeDtyp...]
    unnamed x26 -> x27, local copies, waits for them, and re-layouts: 1.23 us -> 11.4 us
    dot_general x4 -> x0, matrix products: 8.28 us -> none  [the longest x1 4.46 us: body(): jnp.einsum('nij,nj->ni', matrix, picked, preferred_element_type=jnp.float32)]
    gather x2 -> x0, local copies, waits for them, and re-layouts: 1.42 us -> none  [the longest x1 0.71 us: body(): picked_dual = dual_rows[rows]]
where the time goes in v1:
time: 32.8 us; the launch traced here: 32.4 us
  Pallas kernels  18.3 us (56%)
  local copies, waits for them, and re-layouts  11.4 us (35%)
  between operations  2.6 us (8%)
    pallas_call x1, Pallas kernels, body(): pl.pallas_call(functools.partial(kernel, n_row), out_shape=(jax.ShapeDtyp...  18.3 us
    unnamed x27, local copies, waits for them, and re-layouts  11.4 us

profile of v1, /device:TPU:0, one launch (start us, length us, event | category | flops | bytes accessed | tf_op | source)
XLA Modules:
  0.0 32.4 jit_solution(10729460572650971082)
XLA Ops:
  2.6 0.0 copy-start
  2.6 2.2 %copy-done = bf16[1,1,128,128,128]{4,3,2,1,0:T(8,128)(2,1)S(1)} copy-done((bf16[1,1,128,128,128]{4,3,2,1,0:T(8,128)(2,1)S(1)}, bf16[1,1,128,128,128]{4,3,2,1,0:T(8,128)(2,1)}, u32[]{:S(2)}) %copy-start) | copy-done | bytes 4194328
  4.8 0.0 copy-start.1
  4.8 0.7 %copy-done.1 = f32[8,128]{1,0:T(8,128)S(1)} copy-done((f32[8,128]{1,0:T(8,128)S(1)}, f32[8,128]{1,0:T(8,128)}, u32[]{:S(2)}) %copy-start.1) | copy-done | bytes 4120
  5.4 0.0 copy-start.2
  5.5 0.7 %copy-done.2 = f32[8,128]{1,0:T(8,128)S(1)} copy-done((f32[8,128]{1,0:T(8,128)S(1)}, f32[8,128]{1,0:T(8,128)}, u32[]{:S(2)}) %copy-start.2) | copy-done | bytes 4120
  6.1 0.0 copy-start.3
  6.1 0.7 %copy-done.3 = f32[8,128]{1,0:T(8,128)S(1)} copy-done((f32[8,128]{1,0:T(8,128)S(1)}, f32[8,128]{1,0:T(8,128)}, u32[]{:S(2)}) %copy-start.3) | copy-done | bytes 4120
  6.8 0.0 copy-start.4
  6.8 0.7 %copy-done.4 = f32[8,128]{1,0:T(8,128)S(1)} copy-done((f32[8,128]{1,0:T(8,128)S(1)}, f32[8,128]{1,0:T(8,128)}, u32[]{:S(2)}) %copy-start.4) | copy-done | bytes 4120
  7.5 0.0 copy-start.5
  7.5 0.7 %copy-done.5 = f32[8,128]{1,0:T(8,128)S(1)} copy-done((f32[8,128]{1,0:T(8,128)S(1)}, f32[8,128]{1,0:T(8,128)}, u32[]{:S(2)}) %copy-start.5) | copy-done | bytes 4120
  8.2 0.0 copy-start.6
  8.2 0.7 %copy-done.6 = s32[8,128]{1,0:T(8,128)S(1)} copy-done((s32[8,128]{1,0:T(8,128)S(1)}, s32[8,128]{1,0:T(8,128)}, u32[]{:S(2)}) %copy-start.6) | copy-done | bytes 4120
  8.9 0.0 copy-start.7
  8.9 0.7 %copy-done.7 = f32[4,128]{1,0:T(4,128)S(1)} copy-done((f32[4,128]{1,0:T(4,128)S(1)}, f32[4,128]{1,0:T(4,128)}, u32[]{:S(2)}) %copy-start.7) | copy-done | bytes 2072
  9.6 0.7 %copy-done.8 = f32[4,128]{1,0:T(4,128)S(1)} copy-done((f32[4,128]{1,0:T(4,128)S(1)}, f32[4,128]{1,0:T(4,128)}, u32[]{:S(2)}) %copy-start.8) | copy-done | bytes 2072
  10.3 0.7 %copy-done.9 = s32[4,128]{1,0:T(4,128)S(1)} copy-done((s32[4,128]{1,0:T(4,128)S(1)}, s32[4,128]{1,0:T(4,128)}, u32[]{:S(2)}) %copy-start.9) | copy-done | bytes 2072
  10.9 0.7 %copy-done.10 = s32[1,1,128]{2,1,0:T(1,128)S(1)} copy-done((s32[1,1,128]{2,1,0:T(1,128)S(1)}, s32[1,1,128]{2,1,0:T(1,128)}, u32[]{:S(2)}) %copy-start.10) | copy-done | bytes 536
  11.6 0.7 %copy-done.11 = s32[1,1,128]{2,1,0:T(1,128)S(1)} copy-done((s32[1,1,128]{2,1,0:T(1,128)S(1)}, s32[1,1,128]{2,1,0:T(1,128)}, u32[]{:S(2)}) %copy-start.11) | copy-done | bytes 536
  12.2 18.3 %shard_map.166 = (f32[4,128]{1,0:T(4,128)S(1)}, f32[8,128]{1,0:T(8,128)S(1)}, f32[8,128]{1,0:T(8,128)S(1)}) custom-call(bf16[1,1,128,128,128]{4,3,2,1,0:T(8,128)(2,1)S(1)} %copy-done, s32[1,1,128]{2,1,0:T(1,128)S(1)} %copy-done.10, s32[1,1,128]{2,1,0:T(1,128)S(1)} %copy-done.11, s32[1,1]{1,0:T(1,128)S(6)} %copy.21.block_counts, f32[8,128]{1,0:T(8,128)S(1)} %copy-done.1, ...), custom_call_target="tpu_custom_call" | custom-call | tf_op jit(solution)/shard_map/pallas_call | solution.py:272
  30.6 0.6 %copy.24 = f32[4,128]{1,0:T(4,128)} copy(f32[4,128]{1,0:T(4,128)S(1)} %get-tuple-element.6) | data formatting | bytes 4096
  31.2 0.6 %copy.25 = f32[8,128]{1,0:T(8,128)} copy(f32[8,128]{1,0:T(8,128)S(1)} %get-tuple-element.7) | data formatting | bytes 8192
  31.8 0.6 %copy.26 = f32[8,128]{1,0:T(8,128)} copy(f32[8,128]{1,0:T(8,128)S(1)} %get-tuple-element.8) | data formatting | bytes 8192
  (4 shorter events, 0.0 us)
Async XLA Ops:
  2.6 2.2 %copy-start = (bf16[1,1,128,128,128]{4,3,2,1,0:T(8,128)(2,1)S(1)}, bf16[1,1,128,128,128]{4,3,2,1,0:T(8,128)(2,1)}, u32[]{:S(2)}) copy-start(bf16[1,1,128,128,128]{4,3,2,1,0:T(8,128)(2,1)} %blocks.1) | copy-start | bytes 12582916
  4.8 0.7 %copy-start.1 = (f32[8,128]{1,0:T(8,128)S(1)}, f32[8,128]{1,0:T(8,128)}, u32[]{:S(2)}) copy-start(f32[8,128]{1,0:T(8,128)} %primal.1) | copy-start | bytes 12292
  5.4 0.7 %copy-start.2 = (f32[8,128]{1,0:T(8,128)S(1)}, f32[8,128]{1,0:T(8,128)}, u32[]{:S(2)}) copy-start(f32[8,128]{1,0:T(8,128)} %primal_bar.1) | copy-start | bytes 12292
  6.1 0.7 %copy-start.3 = (f32[8,128]{1,0:T(8,128)S(1)}, f32[8,128]{1,0:T(8,128)}, u32[]{:S(2)}) copy-start(f32[8,128]{1,0:T(8,128)} %cost_vec.1) | copy-start | bytes 12292
  6.8 0.7 %copy-start.4 = (f32[8,128]{1,0:T(8,128)S(1)}, f32[8,128]{1,0:T(8,128)}, u32[]{:S(2)}) copy-start(f32[8,128]{1,0:T(8,128)} %lower.1) | copy-start | bytes 12292
  7.5 0.7 %copy-start.5 = (f32[8,128]{1,0:T(8,128)S(1)}, f32[8,128]{1,0:T(8,128)}, u32[]{:S(2)}) copy-start(f32[8,128]{1,0:T(8,128)} %upper.1) | copy-start | bytes 12292
  8.2 0.7 %copy-start.6 = (s32[8,128]{1,0:T(8,128)S(1)}, s32[8,128]{1,0:T(8,128)}, u32[]{:S(2)}) copy-start(s32[8,128]{1,0:T(8,128)} %bound_kind.1) | copy-start | bytes 12292
  8.9 0.7 %copy-start.7 = (f32[4,128]{1,0:T(4,128)S(1)}, f32[4,128]{1,0:T(4,128)}, u32[]{:S(2)}) copy-start(f32[4,128]{1,0:T(4,128)} %dual.1) | copy-start | bytes 6148
  9.6 0.7 %copy-start.8 = (f32[4,128]{1,0:T(4,128)S(1)}, f32[4,128]{1,0:T(4,128)}, u32[]{:S(2)}) copy-start(f32[4,128]{1,0:T(4,128)} %rhs.1) | copy-start | bytes 6148
  10.2 0.7 %copy-start.9 = (s32[4,128]{1,0:T(4,128)S(1)}, s32[4,128]{1,0:T(4,128)}, u32[]{:S(2)}) copy-start(s32[4,128]{1,0:T(4,128)} %row_kind.1) | copy-start | bytes 6148
  10.9 0.7 %copy-start.10 = (s32[1,1,128]{2,1,0:T(1,128)S(1)}, s32[1,1,128]{2,1,0:T(1,128)}, u32[]{:S(2)}) copy-start(s32[1,1,128]{2,1,0:T(1,128)} %block_rows.1) | copy-start | bytes 1540
  11.6 0.7 %copy-start.11 = (s32[1,1,128]{2,1,0:T(1,128)S(1)}, s32[1,1,128]{2,1,0:T(1,128)}, u32[]{:S(2)}) copy-start(s32[1,1,128]{2,1,0:T(1,128)} %block_cols.1) | copy-start | bytes 1540

commit v2 on v1

--- a/solution.py
+++ b/solution.py
@@ -9,6 +9,7 @@
 
 MESH = pl.DeviceIdType.MESH
 BLOCK_CHUNKS = 4
+VMEM_BYTES = 64 * 1024 * 1024
 
 
 def kernel(
@@ -263,21 +264,45 @@
     b_copy.wait()
 
 
+def hand_out_kernel(dual_v, primal_v, bar_v, dual_out, primal_out, bar_out, sem):
+    copies = [
+        pltpu.make_async_copy(src, dst, sem.at[i])
+        for i, (src, dst) in enumerate(
+            ((dual_v, dual_out), (primal_v, primal_out), (bar_v, bar_out))
+        )
+    ]
+    for copy in copies:
+        copy.start()
+    for copy in copies:
+        copy.wait()
+
+
+def hand_out(*results):
+    return pl.pallas_call(
+        hand_out_kernel,
+        out_shape=tuple(jax.ShapeDtypeStruct(a.shape, a.dtype) for a in results),
+        in_specs=[pl.BlockSpec(memory_space=pltpu.HBM)] * 3,
+        out_specs=[pl.BlockSpec(memory_space=pltpu.HBM)] * 3,
+        scratch_shapes=[pltpu.SemaphoreType.DMA((3,))],
+        compiler_params=pltpu.CompilerParams(vmem_limit_bytes=VMEM_BYTES),
+    )(*results)
+
+
 def body(n_row, *args):
     blocks, block_rows, primal, dual = args[0], args[1], args[4], args[6]
     slots, size = blocks.shape[2], blocks.shape[3]
     xb, yb = primal.shape[0], dual.shape[0]
     f32, i32 = jnp.float32, jnp.int32
     dma = pltpu.SemaphoreType.DMA
-    return pl.pallas_call(
+    results = pl.pallas_call(
         functools.partial(kernel, n_row),
         out_shape=(
             jax.ShapeDtypeStruct((yb, size), f32),
             jax.ShapeDtypeStruct((xb, size), f32),
             jax.ShapeDtypeStruct((xb, size), f32),
         ),
-        in_specs=[pl.BlockSpec(memory_space=pl.ANY)] * len(args),
-        out_specs=[pl.BlockSpec(memory_space=pl.ANY)] * 3,
+        in_specs=[pl.BlockSpec(memory_space=pltpu.HBM)] * len(args),
+        out_specs=[pl.BlockSpec(memory_space=pltpu.HBM)] * 3,
         scratch_shapes=[
             pltpu.VMEM((slots, size, size), jnp.bfloat16),
             pltpu.SMEM((1, slots), i32),
@@ -307,9 +332,10 @@
             dma((n_row,)),
         ],
         compiler_params=pltpu.CompilerParams(
-            collective_id=0, has_side_effects=True, vmem_limit_bytes=32 * 1024 * 1024
+            collective_id=0, has_side_effects=True, vmem_limit_bytes=VMEM_BYTES
         ),
     )(*args)
+    return hand_out(*results)
 
 
 def solution(mesh):

time: 32.8 us -> 22.8 us (0.70)
  local copies, waits for them, and re-layouts: 11.4 us -> 0 us
  Pallas kernels: 18.3 us -> 20.1 us
    unnamed x27 -> x0, local copies, waits for them, and re-layouts: 11.4 us -> none
    pallas_call x0 -> x1, Pallas kernels: none -> 1.44 us  [hand_out(): pl.pallas_call(hand_out_kernel, out_shape=tuple((jax.ShapeDtypeStruct(a.s...]
where the time goes in v2:
time: 22.8 us; the launch traced here: 22.6 us
  Pallas kernels  20.1 us (88%)
  between operations  2.58 us (11%)
    pallas_call x1, Pallas kernels, body(): pl.pallas_call(functools.partial(kernel, n_row), out_shape=(jax.ShapeDtyp...  18.6 us
    pallas_call x1, Pallas kernels, hand_out(): pl.pallas_call(hand_out_kernel, out_shape=tuple((jax.ShapeDtypeStruct(a.s...  1.44 us

profile of v2, /device:TPU:0, one launch (start us, length us, event | category | flops | bytes accessed | tf_op | source)
XLA Modules:
  0.0 22.6 jit_solution(16919307409224068576)
XLA Ops:
  2.6 18.6 %shard_map.166 = (f32[4,128]{1,0:T(4,128)}, f32[8,128]{1,0:T(8,128)}, f32[8,128]{1,0:T(8,128)}) custom-call(bf16[1,1,128,128,128]{4,3,2,1,0:T(8,128)(2,1)} %blocks.1, s32[1,1,128]{2,1,0:T(1,128)} %block_rows.1, s32[1,1,128]{2,1,0:T(1,128)} %block_cols.1, s32[1,1]{1,0:T(1,128)S(6)} %copy.18.block_counts, f32[8,128]{1,0:T(8,128)} %primal.1, ...), custom_call_target="tpu_custom_call" | custom-call | tf_op jit(solution)/shard_map/pallas_call | solution.py:297
  21.2 1.4 %shard_map.167 = (f32[4,128]{1,0:T(4,128)}, f32[8,128]{1,0:T(8,128)}, f32[8,128]{1,0:T(8,128)}) custom-call(f32[4,128]{1,0:T(4,128)} %get-tuple-element.6.dual_v, f32[8,128]{1,0:T(8,128)} %get-tuple-element.7.primal_v, f32[8,128]{1,0:T(8,128)} %get-tuple-element.8.bar_v), custom_call_target="tpu_custom_call" | custom-call | tf_op jit(solution)/shard_map/pallas_call | solution.py:281

commit v3 on v2

--- a/solution.py
+++ b/solution.py
@@ -9,7 +9,7 @@
 
 MESH = pl.DeviceIdType.MESH
 BLOCK_CHUNKS = 4
-VMEM_BYTES = 64 * 1024 * 1024
+VMEM_BYTES = 32 * 1024 * 1024
 
 
 def kernel(
@@ -48,8 +48,6 @@
     yall,
     kty,
     pieces,
-    out_d,
-    out_p,
     local_sem,
     blk_sem,
     x_send,
@@ -73,6 +71,31 @@
         return copy
 
     x_copy = local(primal_bar, xall.at[mine], 0)
+
+    def peer(k):
+        if n_row > 8:
+            return lax.rem(r + k, n_row)
+        other = r
+        for b in (1, 2, 4):
+            if k & b:
+                other = other + b * (1 - 2 * lax.rem(r // b, 2))
+        return other
+
+    def for_peers(do):
+        if n_row <= 8:
+            for k in range(n_row - 1, 0, -1):
+                do(k)
+        else:
+            lax.fori_loop(1, n_row, lambda k, carry: (do(k), carry)[1], 0)
+
+    barrier = pltpu.get_barrier_semaphore()
+    for_peers(
+        lambda k: pl.semaphore_signal(
+            barrier, inc=1, device_id={"row": peer(k)}, device_id_type=MESH
+        )
+    )
+    pl.semaphore_signal(barrier, inc=1, device_id={"col": 1 - c}, device_id_type=MESH)
+
     dual_copies = [
         local(dual, dual_v.at[0], 1),
         local(rhs, dual_v.at[1], 2),
@@ -99,23 +122,6 @@
         local(primal_step, pstep_s, 13),
     ]
 
-    def peer(k):
-        return lax.rem(r + k, n_row)
-
-    def for_peers(do):
-        if n_row <= 8:
-            for k in range(1, n_row):
-                do(k)
-        else:
-            lax.fori_loop(1, n_row, lambda k, carry: (do(k), carry)[1], 0)
-
-    barrier = pltpu.get_barrier_semaphore()
-    for_peers(
-        lambda k: pl.semaphore_signal(
-            barrier, inc=1, device_id={"row": peer(k)}, device_id_type=MESH
-        )
-    )
-    pl.semaphore_signal(barrier, inc=1, device_id={"col": 1 - c}, device_id_type=MESH)
     pl.semaphore_wait(barrier, n_row)
 
     def x_remote(k):
@@ -184,7 +190,7 @@
         )
 
     acc = jnp.zeros((4 * yb, 2 * size), jnp.float32)
-    acc = lax.fori_loop(0, slots // 4, forward, acc, unroll=8)
+    acc = lax.fori_loop(0, slots // 4, forward, acc, unroll=16)
     total = acc[: 2 * yb, :size] + acc[2 * yb :, size:]
     for h in range(2):
         part[0, h] = total[h * yb : (h + 1) * yb]
@@ -193,12 +199,13 @@
     pack_copy.wait_recv()
     part_copy.wait_recv()
 
+    news = []
     for h in range(2):
         moved = packed[h, 0] - dstep * (part[0, h] + part[1, h])
         new = jnp.maximum(moved, packed[h, 1])
-        out_d[h] = new
+        news.append(new)
         yall[h * yb : (h + 1) * yb, :] = new.astype(jnp.bfloat16).astype(jnp.float32)
-    d_copy = local(out_d.at[c], dual_out, 14)
+    dual_out[...] = jnp.where(c == 0, news[0], news[1])
 
     def masked(n):
         live_col = jnp.where(n < count, cols_s[0, n], -1)
@@ -212,7 +219,7 @@
 
     if n_row <= 8:
         acc = jnp.zeros((xb * n_row, size), jnp.float32)
-        kty[...] = lax.fori_loop(0, slots // 2, backward, acc, unroll=8)
+        kty[...] = lax.fori_loop(0, slots // 2, backward, acc, unroll=32)
     else:
         kty[...] = jnp.zeros_like(kty)
 
@@ -250,18 +257,13 @@
     moved = old - pstep_s[0] * (primal_v[1] - total)
     moved = jnp.where((kind == 1) | (kind == 3), jnp.maximum(moved, primal_v[2]), moved)
     new = jnp.where((kind == 2) | (kind == 3), jnp.minimum(moved, primal_v[3]), moved)
-    out_p[0] = new
-    out_p[1] = 2.0 * new - old
-    p_copy = local(out_p.at[0], primal_out, 15)
-    b_copy = local(out_p.at[1], bar_out, 16)
+    primal_out[...] = new
+    bar_out[...] = 2.0 * new - old
 
     for_peers(lambda k: x_remote(k).wait_send())
     pack_copy.wait_send()
     part_copy.wait_send()
     for_peers(lambda k: t_remote(k).wait_send())
-    d_copy.wait()
-    p_copy.wait()
-    b_copy.wait()
 
 
 def hand_out_kernel(dual_v, primal_v, bar_v, dual_out, primal_out, bar_out, sem):
@@ -281,7 +283,7 @@
     return pl.pallas_call(
         hand_out_kernel,
         out_shape=tuple(jax.ShapeDtypeStruct(a.shape, a.dtype) for a in results),
-        in_specs=[pl.BlockSpec(memory_space=pltpu.HBM)] * 3,
+        in_specs=[pl.BlockSpec(memory_space=pltpu.VMEM)] * 3,
         out_specs=[pl.BlockSpec(memory_space=pltpu.HBM)] * 3,
         scratch_shapes=[pltpu.SemaphoreType.DMA((3,))],
         compiler_params=pltpu.CompilerParams(vmem_limit_bytes=VMEM_BYTES),
@@ -297,12 +299,12 @@
     results = pl.pallas_call(
         functools.partial(kernel, n_row),
         out_shape=(
-            jax.ShapeDtypeStruct((yb, size), f32),
-            jax.ShapeDtypeStruct((xb, size), f32),
-            jax.ShapeDtypeStruct((xb, size), f32),
+            pltpu.VMEM((yb, size), f32),
+            pltpu.VMEM((xb, size), f32),
+            pltpu.VMEM((xb, size), f32),
         ),
         in_specs=[pl.BlockSpec(memory_space=pltpu.HBM)] * len(args),
-        out_specs=[pl.BlockSpec(memory_space=pltpu.HBM)] * 3,
+        out_specs=[pl.BlockSpec(memory_space=pltpu.VMEM)] * 3,
         scratch_shapes=[
             pltpu.VMEM((slots, size, size), jnp.bfloat16),
             pltpu.SMEM((1, slots), i32),
@@ -320,9 +322,7 @@
             pltpu.VMEM((2 * yb, size), f32),
             pltpu.VMEM((n_row * xb, size), f32),
             pltpu.VMEM((n_row, xb, size), f32),
-            pltpu.VMEM((2, yb, size), f32),
-            pltpu.VMEM((2, xb, size), f32),
-            dma((17,)),
+            dma((14,)),
             dma((BLOCK_CHUNKS,)),
             dma((n_row,)),
             dma((n_row,)),
@@ -334,7 +334,7 @@
         compiler_params=pltpu.CompilerParams(
             collective_id=0, has_side_effects=True, vmem_limit_bytes=VMEM_BYTES
         ),
-    )(*args)
+    )(*[a if a.size == 1 else pltpu.with_memory_space_constraint(a, pltpu.HBM) for a in args])
     return hand_out(*results)
 
 

time: 22.8 us -> 20.1 us (0.88)
  Pallas kernels: 20.1 us -> 17.4 us
    pallas_call x1, Pallas kernels: 18.6 us -> 16.7 us  [body(): pl.pallas_call(functools.partial(kernel, n_row), out_shape=(pltpu.VMEM((y...]
    pallas_call x1, Pallas kernels: 1.44 us -> 0.63 us  [hand_out(): pl.pallas_call(hand_out_kernel, out_shape=tuple((jax.ShapeDtypeStruct(a.s...]
where the time goes in v3:
time: 20.1 us; the launch traced here: 19.9 us
  Pallas kernels  17.4 us (87%)
  between operations  2.58 us (13%)
    pallas_call x1, Pallas kernels, body(): pl.pallas_call(functools.partial(kernel, n_row), out_shape=(pltpu.VMEM((y...  16.7 us
    pallas_call x1, Pallas kernels, hand_out(): pl.pallas_call(hand_out_kernel, out_shape=tuple((jax.ShapeDtypeStruct(a.s...  0.63 us

profile of v3, /device:TPU:0, one launch (start us, length us, event | category | flops | bytes accessed | tf_op | source)
XLA Modules:
  0.0 19.9 jit_solution(11214584192736543976)
XLA Ops:
  2.6 16.7 %shard_map.166 = (f32[4,128]{1,0:T(4,128)S(1)}, f32[8,128]{1,0:T(8,128)S(1)}, f32[8,128]{1,0:T(8,128)S(1)}) custom-call(bf16[1,1,128,128,128]{4,3,2,1,0:T(8,128)(2,1)} %blocks.1, s32[1,1,128]{2,1,0:T(1,128)} %block_rows.1, s32[1,1,128]{2,1,0:T(1,128)} %block_cols.1, s32[1,1]{1,0:T(1,128)S(6)} %copy.18.block_counts, f32[8,128]{1,0:T(8,128)} %primal.1, ...), custom_call_target="tpu_custom_call" | custom-call | tf_op jit(solution)/shard_map/pallas_call | solution.py:299
  19.3 0.6 %shard_map.167 = (f32[4,128]{1,0:T(4,128)}, f32[8,128]{1,0:T(8,128)}, f32[8,128]{1,0:T(8,128)}) custom-call(f32[4,128]{1,0:T(4,128)S(1)} %get-tuple-element.6.dual_v, f32[8,128]{1,0:T(8,128)S(1)} %get-tuple-element.7.primal_v, f32[8,128]{1,0:T(8,128)S(1)} %get-tuple-element.8.bar_v), custom_call_target="tpu_custom_call" | custom-call | tf_op jit(solution)/shard_map/pallas_call | solution.py:283

commit v4 on v3

--- a/solution.py
+++ b/solution.py
@@ -9,6 +9,8 @@
 
 MESH = pl.DeviceIdType.MESH
 BLOCK_CHUNKS = 4
+KX_SLOTS = 16
+KTY_SLOTS = 16
 VMEM_BYTES = 32 * 1024 * 1024
 
 
@@ -33,6 +35,7 @@
     primal_out,
     bar_out,
     blk,
+    turned,
     rows_s,
     cols_s,
     count_s,
@@ -161,8 +164,13 @@
     count = count_s[0, 0]
     row_iota = lax.broadcasted_iota(jnp.int32, (2 * yb, size), 0)
     col_iota = lax.broadcasted_iota(jnp.int32, (xb * n_row, size), 0)
-    for copy in blk_copies:
-        copy.wait()
+    def turn(n, carry):
+        turned[n] = blk[n].T
+        return carry
+
+    for k in range(BLOCK_CHUNKS):
+        blk_copies[k].wait()
+        lax.fori_loop(k * per_chunk, (k + 1) * per_chunk, turn, 0, unroll=8)
     for_peers(lambda k: x_remote(k).wait_recv())
 
     def picked(n):
@@ -170,28 +178,13 @@
         return jnp.where(row_iota == live_row, xall[pl.ds(cols_s[0, n], 1), :], 0.0)
 
     def forward(q, acc):
-        n = 4 * q
-        left = jnp.concatenate(
-            [
-                jnp.concatenate([picked(n), picked(n + 1)], 1),
-                jnp.concatenate([picked(n + 2), picked(n + 3)], 1),
-            ],
-            0,
-        ).astype(jnp.bfloat16)
-        right = jnp.concatenate(
-            [
-                jnp.concatenate([blk[n], blk[n + 1]], 1),
-                jnp.concatenate([blk[n + 2], blk[n + 3]], 1),
-            ],
-            0,
-        )
-        return acc + lax.dot_general(
-            left, right, (((1,), (1,)), ((), ())), preferred_element_type=jnp.float32
-        )
-
-    acc = jnp.zeros((4 * yb, 2 * size), jnp.float32)
-    acc = lax.fori_loop(0, slots // 4, forward, acc, unroll=16)
-    total = acc[: 2 * yb, :size] + acc[2 * yb :, size:]
+        n = KX_SLOTS * q
+        left = jnp.concatenate([picked(n + i).astype(jnp.bfloat16) for i in range(KX_SLOTS)], 1)
+        right = turned[pl.ds(n, KX_SLOTS)].reshape(KX_SLOTS * size, size)
+        return acc + jnp.dot(left, right, preferred_element_type=jnp.float32)
+
+    acc = jnp.zeros((2 * yb, size), jnp.float32)
+    total = lax.fori_loop(0, slots // KX_SLOTS, forward, acc, unroll=4)
     for h in range(2):
         part[0, h] = total[h * yb : (h + 1) * yb]
     part_copy = to_pair(part.at[0], part.at[1], 1)
@@ -212,14 +205,14 @@
         return jnp.where(col_iota == live_col, yall[pl.ds(rows_s[0, n], 1), :], 0.0)
 
     def backward(q, acc):
-        n = 2 * q
-        left = jnp.concatenate([masked(n), masked(n + 1)], 1).astype(jnp.bfloat16)
-        right = jnp.concatenate([blk[n], blk[n + 1]], 0)
+        n = KTY_SLOTS * q
+        left = jnp.concatenate([masked(n + i).astype(jnp.bfloat16) for i in range(KTY_SLOTS)], 1)
+        right = blk[pl.ds(n, KTY_SLOTS)].reshape(KTY_SLOTS * size, size)
         return acc + jnp.dot(left, right, preferred_element_type=jnp.float32)
 
     if n_row <= 8:
         acc = jnp.zeros((xb * n_row, size), jnp.float32)
-        kty[...] = lax.fori_loop(0, slots // 2, backward, acc, unroll=32)
+        kty[...] = lax.fori_loop(0, slots // KTY_SLOTS, backward, acc, unroll=4)
     else:
         kty[...] = jnp.zeros_like(kty)
 
@@ -227,7 +220,7 @@
             kty[...] = backward(q, kty[...])
             return carry
 
-        lax.fori_loop(0, slots // 2, into, 0)
+        lax.fori_loop(0, slots // KTY_SLOTS, into, 0)
 
     def t_remote(k):
         theirs = pl.ds(pl.multiple_of(peer(k) * xb, xb), xb)
@@ -306,6 +299,7 @@
         in_specs=[pl.BlockSpec(memory_space=pltpu.HBM)] * len(args),
         out_specs=[pl.BlockSpec(memory_space=pltpu.VMEM)] * 3,
         scratch_shapes=[
+            pltpu.VMEM((slots, size, size), jnp.bfloat16),
             pltpu.VMEM((slots, size, size), jnp.bfloat16),
             pltpu.SMEM((1, slots), i32),
             pltpu.SMEM((1, slots), i32),

time: 20.1 us -> 19.6 us (0.975)
  Pallas kernels: 17.4 us -> 16.9 us
    pallas_call x1, Pallas kernels: 16.7 us -> 16.2 us  [body(): pl.pallas_call(functools.partial(kernel, n_row), out_shape=(pltpu.VMEM((y...]
where the time goes in v4:
time: 19.6 us; the launch traced here: 19.4 us
  Pallas kernels  16.9 us (86%)
  between operations  2.58 us (13%)
    pallas_call x1, Pallas kernels, body(): pl.pallas_call(functools.partial(kernel, n_row), out_shape=(pltpu.VMEM((y...  16.2 us
    pallas_call x1, Pallas kernels, hand_out(): pl.pallas_call(hand_out_kernel, out_shape=tuple((jax.ShapeDtypeStruct(a.s...  0.63 us

profile of v4, /device:TPU:0, one launch (start us, length us, event | category | flops | bytes accessed | tf_op | source)
XLA Modules:
  0.0 19.4 jit_solution(6831084793479508993)
XLA Ops:
  2.6 16.2 %shard_map.166 = (f32[4,128]{1,0:T(4,128)S(1)}, f32[8,128]{1,0:T(8,128)S(1)}, f32[8,128]{1,0:T(8,128)S(1)}) custom-call(bf16[1,1,128,128,128]{4,3,2,1,0:T(8,128)(2,1)} %blocks.1, s32[1,1,128]{2,1,0:T(1,128)} %block_rows.1, s32[1,1,128]{2,1,0:T(1,128)} %block_cols.1, s32[1,1]{1,0:T(1,128)S(6)} %copy.18.block_counts, f32[8,128]{1,0:T(8,128)} %primal.1, ...), custom_call_target="tpu_custom_call" | custom-call | tf_op jit(solution)/shard_map/pallas_call | solution.py:292
  18.8 0.6 %shard_map.167 = (f32[4,128]{1,0:T(4,128)}, f32[8,128]{1,0:T(8,128)}, f32[8,128]{1,0:T(8,128)}) custom-call(f32[4,128]{1,0:T(4,128)S(1)} %get-tuple-element.6.dual_v, f32[8,128]{1,0:T(8,128)S(1)} %get-tuple-element.7.primal_v, f32[8,128]{1,0:T(8,128)S(1)} %get-tuple-element.8.bar_v), custom_call_target="tpu_custom_call" | custom-call | tf_op jit(solution)/shard_map/pallas_call | solution.py:276

commit v5 on v4

--- a/solution.py
+++ b/solution.py
@@ -9,6 +9,8 @@
 
 MESH = pl.DeviceIdType.MESH
 BLOCK_CHUNKS = 4
+FORWARD_GROUPS = ((0, 1, 2, 3), (4, 5), (6, 7))
+BACKWARD_GROUPS = ((7, 6), (5, 4), (3, 2, 1, 0))
 KX_SLOTS = 16
 KTY_SLOTS = 16
 VMEM_BYTES = 32 * 1024 * 1024
@@ -36,6 +38,11 @@
     bar_out,
     blk,
     turned,
+    placed,
+    lane_v,
+    order_v,
+    order_s,
+    pieces_x,
     rows_s,
     cols_s,
     count_s,
@@ -52,6 +59,7 @@
     kty,
     pieces,
     local_sem,
+    order_sem,
     blk_sem,
     x_send,
     x_recv,
@@ -108,6 +116,8 @@
     index_copies = [
         local(block_rows.at[0], rows_s, 5),
         local(block_cols.at[0], cols_s, 6),
+        local(block_cols.at[0], lane_v.at[0], 14),
+        local(block_rows.at[0], lane_v.at[1], 15),
         local(block_counts, count_s, 7),
     ]
     blk_copies = []
@@ -164,27 +174,101 @@
     count = count_s[0, 0]
     row_iota = lax.broadcasted_iota(jnp.int32, (2 * yb, size), 0)
     col_iota = lax.broadcasted_iota(jnp.int32, (xb * n_row, size), 0)
+    by_owner = n_row <= 8
+    cap = slots // n_row
+
+    def owner_slots(k):
+        return pl.multiple_of(peer(k) * cap, cap) if k else pl.multiple_of(r * cap, cap)
+
+    if by_owner:
+        cols_row = lane_v[0]
+        here = lax.broadcasted_iota(jnp.int32, (slots, slots), 0)
+        lane = lax.broadcasted_iota(jnp.int32, (slots, slots), 1)
+        owner = jnp.where(lane[:1] < count, cols_row // xb, -1)
+        owner_of = jnp.broadcast_to(owner, (slots, slots)).T
+        same = (owner_of == owner) & (here < lane)
+        rank = jnp.sum(same.astype(jnp.int32), axis=0, keepdims=True)
+        place = jnp.where(owner < 0, -1, owner * cap + rank)
+        hit = jnp.broadcast_to(place, (slots, slots)).T == lane
+        rows_of = jnp.broadcast_to(lane_v[1], (slots, slots)).T
+        inner_of = jnp.broadcast_to(lax.rem(cols_row, xb), (slots, slots)).T
+
+        def placed_at(values):
+            return jnp.sum(jnp.where(hit, values, 0), axis=0, keepdims=True)
+
+        full = placed_at(jnp.ones_like(here))
+        for i, values in enumerate((here, rows_of, inner_of)):
+            order_v[i : i + 1, :] = placed_at(values)
+        for i in (1, 2):
+            order_v[i + 2 : i + 3, :] = jnp.where(full > 0, order_v[i : i + 1, :], -1)
+        order_copy = pltpu.make_async_copy(order_v, order_s, order_sem)
+        order_copy.start()
+        order_copy.wait()
+
     def turn(n, carry):
-        turned[n] = blk[n].T
+        if by_owner:
+            block = blk[order_s[0, n]]
+            placed[n] = block
+            turned[n] = block.T
+        else:
+            turned[n] = blk[n].T
         return carry
 
-    for k in range(BLOCK_CHUNKS):
-        blk_copies[k].wait()
-        lax.fori_loop(k * per_chunk, (k + 1) * per_chunk, turn, 0, unroll=8)
-    for_peers(lambda k: x_remote(k).wait_recv())
-
-    def picked(n):
-        live_row = jnp.where(n < count, rows_s[0, n], -1)
-        return jnp.where(row_iota == live_row, xall[pl.ds(cols_s[0, n], 1), :], 0.0)
-
-    def forward(q, acc):
-        n = KX_SLOTS * q
-        left = jnp.concatenate([picked(n + i).astype(jnp.bfloat16) for i in range(KX_SLOTS)], 1)
-        right = turned[pl.ds(n, KX_SLOTS)].reshape(KX_SLOTS * size, size)
-        return acc + jnp.dot(left, right, preferred_element_type=jnp.float32)
-
-    acc = jnp.zeros((2 * yb, size), jnp.float32)
-    total = lax.fori_loop(0, slots // KX_SLOTS, forward, acc, unroll=4)
+    for copy in blk_copies:
+        copy.wait()
+    lax.fori_loop(0, slots, turn, 0, unroll=8)
+
+    inner_iota = lax.broadcasted_iota(jnp.int32, (xb, size), 0)
+
+    def owner_forward(k, acc):
+        first = owner_slots(k)
+        lefts = []
+        for i in range(cap):
+            p = first + i
+            x_row = pieces_x[pl.ds(k * xb + order_s[2, p], 1), :]
+            chosen = row_iota == order_s[3, p]
+            lefts.append(jnp.where(chosen, x_row, 0.0).astype(jnp.bfloat16))
+        right = turned[pl.ds(first, cap)].reshape(cap * size, size)
+        return acc + jnp.dot(
+            jnp.concatenate(lefts, 1), right, preferred_element_type=jnp.float32
+        )
+
+    def owner_backward(k):
+        first = owner_slots(k)
+        lefts = []
+        for i in range(cap):
+            p = first + i
+            y_row = yall[pl.ds(order_s[1, p], 1), :]
+            chosen = inner_iota == order_s[4, p]
+            lefts.append(jnp.where(chosen, y_row, 0.0).astype(jnp.bfloat16))
+        right = placed[pl.ds(first, cap)].reshape(cap * size, size)
+        return jnp.dot(jnp.concatenate(lefts, 1), right, preferred_element_type=jnp.float32)
+
+    if by_owner:
+        total = jnp.zeros((2 * yb, size), jnp.float32)
+        for group in FORWARD_GROUPS:
+            for k in group:
+                if k:
+                    x_remote(k).wait_recv()
+                theirs = pl.ds(pl.multiple_of((peer(k) if k else r) * xb, xb), xb)
+                pieces_x[k * xb : (k + 1) * xb, :] = xall[theirs, :]
+            for k in group:
+                total = owner_forward(k, total)
+    else:
+        for_peers(lambda k: x_remote(k).wait_recv())
+
+        def picked(n):
+            live_row = jnp.where(n < count, rows_s[0, n], -1)
+            return jnp.where(row_iota == live_row, xall[pl.ds(cols_s[0, n], 1), :], 0.0)
+
+        def forward(q, acc):
+            n = KX_SLOTS * q
+            left = jnp.concatenate([picked(n + i).astype(jnp.bfloat16) for i in range(KX_SLOTS)], 1)
+            right = turned[pl.ds(n, KX_SLOTS)].reshape(KX_SLOTS * size, size)
+            return acc + jnp.dot(left, right, preferred_element_type=jnp.float32)
+
+        acc = jnp.zeros((2 * yb, size), jnp.float32)
+        total = lax.fori_loop(0, slots // KX_SLOTS, forward, acc, unroll=4)
     for h in range(2):
         part[0, h] = total[h * yb : (h + 1) * yb]
     part_copy = to_pair(part.at[0], part.at[1], 1)
@@ -210,10 +294,7 @@
         right = blk[pl.ds(n, KTY_SLOTS)].reshape(KTY_SLOTS * size, size)
         return acc + jnp.dot(left, right, preferred_element_type=jnp.float32)
 
-    if n_row <= 8:
-        acc = jnp.zeros((xb * n_row, size), jnp.float32)
-        kty[...] = lax.fori_loop(0, slots // KTY_SLOTS, backward, acc, unroll=4)
-    else:
+    if not by_owner:
         kty[...] = jnp.zeros_like(kty)
 
         def into(q, carry):
@@ -223,9 +304,9 @@
         lax.fori_loop(0, slots // KTY_SLOTS, into, 0)
 
     def t_remote(k):
-        theirs = pl.ds(pl.multiple_of(peer(k) * xb, xb), xb)
+        at = k if by_owner else peer(k)
         return pltpu.make_async_remote_copy(
-            src_ref=kty.at[theirs],
+            src_ref=kty.at[pl.ds(pl.multiple_of(at * xb, xb), xb)],
             dst_ref=pieces.at[k],
             send_sem=t_send.at[k],
             recv_sem=t_recv.at[k],
@@ -233,11 +314,21 @@
             device_id_type=MESH,
         )
 
-    for_peers(lambda k: t_remote(k).start())
+    if by_owner:
+        for group in BACKWARD_GROUPS:
+            sums = [owner_backward(k) for k in group]
+            for k, part_sum in zip(group, sums):
+                if k:
+                    kty[k * xb : (k + 1) * xb, :] = part_sum
+                    t_remote(k).start()
+                else:
+                    total = part_sum
+    else:
+        for_peers(lambda k: t_remote(k).start())
+        total = kty[mine, :]
     for copy in primal_copies:
         copy.wait()
-    total = kty[mine, :]
-    if n_row <= 8:
+    if by_owner:
         for k in range(1, n_row):
             t_remote(k).wait_recv()
             total = total + pieces[k]
@@ -301,6 +392,11 @@
         scratch_shapes=[
             pltpu.VMEM((slots, size, size), jnp.bfloat16),
             pltpu.VMEM((slots, size, size), jnp.bfloat16),
+            pltpu.VMEM((slots, size, size), jnp.bfloat16),
+            pltpu.VMEM((2, 1, slots), i32),
+            pltpu.VMEM((8, slots), i32),
+            pltpu.SMEM((8, slots), i32),
+            pltpu.VMEM((n_row * xb, size), f32),
             pltpu.SMEM((1, slots), i32),
             pltpu.SMEM((1, slots), i32),
             pltpu.SMEM((1, 1), i32),
@@ -316,7 +412,8 @@
             pltpu.VMEM((2 * yb, size), f32),
             pltpu.VMEM((n_row * xb, size), f32),
             pltpu.VMEM((n_row, xb, size), f32),
-            dma((14,)),
+            dma((16,)),
+            dma(()),
             dma((BLOCK_CHUNKS,)),
             dma((n_row,)),
             dma((n_row,)),

time: 19.6 us -> 18.3 us (0.934)
  Pallas kernels: 16.9 us -> 15.6 us
    pallas_call x1, Pallas kernels: 16.2 us -> 15 us  [body(): pl.pallas_call(functools.partial(kernel, n_row), out_shape=(pltpu.VMEM((y...]
where the time goes in v5:
time: 18.3 us; the launch traced here: 18.2 us
  Pallas kernels  15.6 us (85%)
  between operations  2.58 us (14%)
    pallas_call x1, Pallas kernels, body(): pl.pallas_call(functools.partial(kernel, n_row), out_shape=(pltpu.VMEM((y...  15 us
    pallas_call x1, Pallas kernels, hand_out(): pl.pallas_call(hand_out_kernel, out_shape=tuple((jax.ShapeDtypeStruct(a.s...  0.63 us

profile of v5, /device:TPU:0, one launch (start us, length us, event | category | flops | bytes accessed | tf_op | source)
XLA Modules:
  0.0 18.2 jit_solution(1834528415660643112)
XLA Ops:
  2.6 15.0 %shard_map.166 = (f32[4,128]{1,0:T(4,128)S(1)}, f32[8,128]{1,0:T(8,128)S(1)}, f32[8,128]{1,0:T(8,128)S(1)}) custom-call(bf16[1,1,128,128,128]{4,3,2,1,0:T(8,128)(2,1)} %blocks.1, s32[1,1,128]{2,1,0:T(1,128)} %block_rows.1, s32[1,1,128]{2,1,0:T(1,128)} %block_cols.1, s32[1,1]{1,0:T(1,128)S(6)} %copy.18.block_counts, f32[8,128]{1,0:T(8,128)} %primal.1, ...), custom_call_target="tpu_custom_call" | custom-call | tf_op jit(solution)/shard_map/pallas_call | solution.py:383
  17.5 0.6 %shard_map.167 = (f32[4,128]{1,0:T(4,128)}, f32[8,128]{1,0:T(8,128)}, f32[8,128]{1,0:T(8,128)}) custom-call(f32[4,128]{1,0:T(4,128)S(1)} %get-tuple-element.6.dual_v, f32[8,128]{1,0:T(8,128)S(1)} %get-tuple-element.7.primal_v, f32[8,128]{1,0:T(8,128)S(1)} %get-tuple-element.8.bar_v), custom_call_target="tpu_custom_call" | custom-call | tf_op jit(solution)/shard_map/pallas_call | solution.py:367

commit v6 on v5

--- a/solution.py
+++ b/solution.py
@@ -9,8 +9,8 @@
 
 MESH = pl.DeviceIdType.MESH
 BLOCK_CHUNKS = 4
-FORWARD_GROUPS = ((0, 1, 2, 3), (4, 5), (6, 7))
-BACKWARD_GROUPS = ((7, 6), (5, 4), (3, 2, 1, 0))
+FORWARD_GROUPS = ((0, 1, 2, 3), (4, 5), (6,), (7,))
+BACKWARD_GROUPS = ((7,), (6,), (5, 4), (3, 2, 1, 0))
 KX_SLOTS = 16
 KTY_SLOTS = 16
 VMEM_BYTES = 32 * 1024 * 1024
@@ -45,9 +45,6 @@
     pieces_x,
     rows_s,
     cols_s,
-    count_s,
-    pstep_s,
-    dstep_s,
     xall,
     dual_v,
     primal_v,
@@ -111,14 +108,10 @@
         local(dual, dual_v.at[0], 1),
         local(rhs, dual_v.at[1], 2),
         local(row_kind, kind_row_v, 3),
-        local(dual_step, dstep_s, 4),
     ]
     index_copies = [
-        local(block_rows.at[0], rows_s, 5),
-        local(block_cols.at[0], cols_s, 6),
-        local(block_cols.at[0], lane_v.at[0], 14),
-        local(block_rows.at[0], lane_v.at[1], 15),
-        local(block_counts, count_s, 7),
+        local(block_cols.at[0], lane_v.at[0] if n_row <= 8 else cols_s, 5),
+        local(block_rows.at[0], lane_v.at[1] if n_row <= 8 else rows_s, 6),
     ]
     blk_copies = []
     for k in range(BLOCK_CHUNKS):
@@ -132,7 +125,6 @@
         local(lower, primal_v.at[2], 10),
         local(upper, primal_v.at[3], 11),
         local(bound_kind, kind_v, 12),
-        local(primal_step, pstep_s, 13),
     ]
 
     pl.semaphore_wait(barrier, n_row)
@@ -152,7 +144,7 @@
 
     for copy in dual_copies:
         copy.wait()
-    dstep = dstep_s[0]
+    dstep = dual_step[0]
     packed[c, 0] = dual_v[0] + dstep * dual_v[1]
     packed[c, 1] = jnp.where(kind_row_v[...] == 1, 0.0, -jnp.inf)
 
@@ -171,7 +163,7 @@
 
     for copy in index_copies:
         copy.wait()
-    count = count_s[0, 0]
+    count = block_counts[0, 0]
     row_iota = lax.broadcasted_iota(jnp.int32, (2 * yb, size), 0)
     col_iota = lax.broadcasted_iota(jnp.int32, (xb * n_row, size), 0)
     by_owner = n_row <= 8
@@ -338,7 +330,7 @@
 
     old = primal_v[0]
     kind = kind_v[...]
-    moved = old - pstep_s[0] * (primal_v[1] - total)
+    moved = old - primal_step[0] * (primal_v[1] - total)
     moved = jnp.where((kind == 1) | (kind == 3), jnp.maximum(moved, primal_v[2]), moved)
     new = jnp.where((kind == 2) | (kind == 3), jnp.minimum(moved, primal_v[3]), moved)
     primal_out[...] = new
@@ -387,7 +379,9 @@
             pltpu.VMEM((xb, size), f32),
             pltpu.VMEM((xb, size), f32),
         ),
-        in_specs=[pl.BlockSpec(memory_space=pltpu.HBM)] * len(args),
+        in_specs=[
+            pl.BlockSpec(memory_space=pltpu.SMEM if a.size == 1 else pltpu.HBM) for a in args
+        ],
         out_specs=[pl.BlockSpec(memory_space=pltpu.VMEM)] * 3,
         scratch_shapes=[
             pltpu.VMEM((slots, size, size), jnp.bfloat16),
@@ -399,9 +393,6 @@
             pltpu.VMEM((n_row * xb, size), f32),
             pltpu.SMEM((1, slots), i32),
             pltpu.SMEM((1, slots), i32),
-            pltpu.SMEM((1, 1), i32),
-            pltpu.SMEM((1,), f32),
-            pltpu.SMEM((1,), f32),
             pltpu.VMEM((n_row * xb, size), f32),
             pltpu.VMEM((2, yb, size), f32),
             pltpu.VMEM((4, xb, size), f32),

time: 18.3 us -> 18.3 us (level)
  no operation moved by 1% of the time
where the time goes in v6:
time: 18.3 us; the launch traced here: 18.2 us
  Pallas kernels  15.6 us (85%)
  between operations  2.58 us (14%)
    pallas_call x1, Pallas kernels, body(): pl.pallas_call(functools.partial(kernel, n_row), out_shape=(pltpu.VMEM((y...  15 us
    pallas_call x1, Pallas kernels, hand_out(): pl.pallas_call(hand_out_kernel, out_shape=tuple((jax.ShapeDtypeStruct(a.s...  0.63 us

profile of v6, /device:TPU:0, one launch (start us, length us, event | category | flops | bytes accessed | tf_op | source)
XLA Modules:
  0.0 18.2 jit_solution(5577957485850314394)
XLA Ops:
  2.6 15.0 %shard_map.166 = (f32[4,128]{1,0:T(4,128)S(1)}, f32[8,128]{1,0:T(8,128)S(1)}, f32[8,128]{1,0:T(8,128)S(1)}) custom-call(bf16[1,1,128,128,128]{4,3,2,1,0:T(8,128)(2,1)} %blocks.1, s32[1,1,128]{2,1,0:T(1,128)} %block_rows.1, s32[1,1,128]{2,1,0:T(1,128)} %block_cols.1, s32[1,1]{1,0:T(1,128)S(6)} %copy.18.block_counts, f32[8,128]{1,0:T(8,128)} %primal.1, ...), custom_call_target="tpu_custom_call" | custom-call | tf_op jit(solution)/shard_map/pallas_call | solution.py:375
  17.5 0.6 %shard_map.167 = (f32[4,128]{1,0:T(4,128)}, f32[8,128]{1,0:T(8,128)}, f32[8,128]{1,0:T(8,128)}) custom-call(f32[4,128]{1,0:T(4,128)S(1)} %get-tuple-element.6.dual_v, f32[8,128]{1,0:T(8,128)S(1)} %get-tuple-element.7.primal_v, f32[8,128]{1,0:T(8,128)S(1)} %get-tuple-element.8.bar_v), custom_call_target="tpu_custom_call" | custom-call | tf_op jit(solution)/shard_map/pallas_call | solution.py:359

commit v7 on v5

--- a/solution.py
+++ b/solution.py
@@ -9,7 +9,7 @@
 
 MESH = pl.DeviceIdType.MESH
 BLOCK_CHUNKS = 4
-FORWARD_GROUPS = ((0, 1, 2, 3), (4, 5), (6, 7))
+FORWARD_GROUPS = ((0, 1), (2, 3), (4, 5), (6,), (7,))
 BACKWARD_GROUPS = ((7, 6), (5, 4), (3, 2, 1, 0))
 KX_SLOTS = 16
 KTY_SLOTS = 16

time: 18.3 us -> 18.2 us (level)
  no operation moved by 1% of the time
where the time goes in v7:
time: 18.2 us; the launch traced here: 18.1 us
  Pallas kernels  15.5 us (85%)
  between operations  2.58 us (14%)
    pallas_call x1, Pallas kernels, body(): pl.pallas_call(functools.partial(kernel, n_row), out_shape=(pltpu.VMEM((y...  14.9 us
    pallas_call x1, Pallas kernels, hand_out(): pl.pallas_call(hand_out_kernel, out_shape=tuple((jax.ShapeDtypeStruct(a.s...  0.63 us

profile of v7, /device:TPU:0, one launch (start us, length us, event | category | flops | bytes accessed | tf_op | source)
XLA Modules:
  0.0 18.1 jit_solution(17934165334994517479)
XLA Ops:
  2.6 14.9 %shard_map.166 = (f32[4,128]{1,0:T(4,128)S(1)}, f32[8,128]{1,0:T(8,128)S(1)}, f32[8,128]{1,0:T(8,128)S(1)}) custom-call(bf16[1,1,128,128,128]{4,3,2,1,0:T(8,128)(2,1)} %blocks.1, s32[1,1,128]{2,1,0:T(1,128)} %block_rows.1, s32[1,1,128]{2,1,0:T(1,128)} %block_cols.1, s32[1,1]{1,0:T(1,128)S(6)} %copy.18.block_counts, f32[8,128]{1,0:T(8,128)} %primal.1, ...), custom_call_target="tpu_custom_call" | custom-call | tf_op jit(solution)/shard_map/pallas_call | solution.py:383
  17.4 0.6 %shard_map.167 = (f32[4,128]{1,0:T(4,128)}, f32[8,128]{1,0:T(8,128)}, f32[8,128]{1,0:T(8,128)}) custom-call(f32[4,128]{1,0:T(4,128)S(1)} %get-tuple-element.6.dual_v, f32[8,128]{1,0:T(8,128)S(1)} %get-tuple-element.7.primal_v, f32[8,128]{1,0:T(8,128)S(1)} %get-tuple-element.8.bar_v), custom_call_target="tpu_custom_call" | custom-call | tf_op jit(solution)/shard_map/pallas_call | solution.py:367
